TPU v7x, 32 devices: a whole 2x2x4 slice. The times are simulated.
32 devices in a mesh: dp: 8 (over y, x, core), fsdp: 4 (over z).
Axes of the slice: x: 2, y: 2, z: 4, core: 2. Of those that a mesh axis runs over, the one named last changes fastest.
Arguments:
- tokens: bfloat16 [32768, 1024], P(('dp', 'fsdp')), may hold values from -6 to 6
- segments: int32 [32768], P(('dp', 'fsdp')), may hold values from 0 to 127, never falling along the last dimension, each value on 1 to 1024 neighbouring positions
- cotangent: bfloat16 [32768, 1024], P(('dp', 'fsdp')), may hold values from -16 to 16
- ln1_gain: bfloat16 [1024], P(('dp', 'fsdp')), may hold values from 0.5 to 1.5
- ln1_bias: bfloat16 [1024], P(('dp', 'fsdp')), may hold values from -1.5 to 1.5
- w_qkv: bfloat16 [1024, 3072], P(('dp', 'fsdp')), may hold values from -0.1875 to 0.1875
- b_qkv: bfloat16 [3072], P(('dp', 'fsdp')), may hold values from -1.5 to 1.5
- w_out: bfloat16 [1024, 1024], P(('dp', 'fsdp')), may hold values from -0.75 to 0.75
- b_out: bfloat16 [1024], P(('dp', 'fsdp')), may hold values from -1.5 to 1.5
- ln2_gain: bfloat16 [1024], P(('dp', 'fsdp')), may hold values from 0.5 to 1.5
- ln2_bias: bfloat16 [1024], P(('dp', 'fsdp')), may hold values from -1.5 to 1.5
- w_fc: bfloat16 [1024, 4096], P(('dp', 'fsdp')), may hold values from -0.1875 to 0.1875
- b_fc: bfloat16 [4096], P(('dp', 'fsdp')), may hold values from -1.5 to 1.5
- w_proj: bfloat16 [4096, 1024], P(('dp', 'fsdp')), may hold values from -0.09375 to 0.09375
- b_proj: bfloat16 [1024], P(('dp', 'fsdp')), may hold values from -1.5 to 1.5
- prefix_embed: bfloat16 [10, 1024], replicated, may hold values from -6 to 6
- w_mid: bfloat16 [1024, 512], replicated, may hold values from -0.1875 to 0.1875
- b_mid: bfloat16 [512], replicated, may hold values from -1.5 to 1.5
- w_kv: bfloat16 [512, 2048], replicated, may hold values from -0.25 to 0.25
- b_kv: bfloat16 [2048], replicated, may hold values from -1.5 to 1.5
Outputs:
- block_out: bfloat16 [32768, 1024], P(('dp', 'fsdp'))
- grad_tokens: bfloat16 [32768, 1024], P(('dp', 'fsdp'))
- grad_embed: float32 [10, 1024], replicated
- grad_mid_w: float32 [1024, 512], replicated
- grad_mid_b: float32 [512], replicated
- grad_kv_w: float32 [512, 2048], replicated
- grad_kv_b: float32 [2048], replicated
Inputs may be any that keep to these rules, and one draw needn't show every extreme that they name: `segments`: segment numbers never fall along the tokens, every number up to the largest occurs, each covers 1 to 1024 tokens and some number exactly 1024; a number may continue across two sequences.
All inputs are finite; a program needn't handle non-finite values.
Results may differ from a plain program's by a relative error of at most 0.013.
Values may be sent and summed in bfloat16 or wider, within the bound.
No kernel may reach another device: no remote copies, remote signals or barrier semaphores. Data moves between devices by JAX's collectives and lax.ppermute only.
A program may use at most 192 MiB of HBM per device.

v0:
```python
import jax
import jax.numpy as jnp
from jax import lax
from jax.sharding import PartitionSpec as P

HEAD = 64
PREFIX = 10
LENGTH = 1024


def layer_norm(values, gain_row, shift_row):
    row_mean = jnp.mean(values, axis=-1, keepdims=True)
    centred = values - row_mean
    spread = jnp.mean(centred * centred, axis=-1, keepdims=True)
    return centred * lax.rsqrt(spread + 1e-05) * gain_row + shift_row


def norm_back(values, gain_row, grad_in):

    def apply_norm(inner_values):
        return layer_norm(inner_values, gain_row, 0.0)

    _, pullback = jax.vjp(apply_norm, values)
    return pullback(grad_in)[0]


def gelu_tanh(values):
    return jax.nn.gelu(values, approximate=True)


def dot_plain(left, right):
    return jnp.dot(left, right, preferred_element_type=jnp.float32)


def dot_first(left, right):
    return lax.dot_general(
        left, right, (((0,), (0,)), ((), ())), preferred_element_type=jnp.float32
    )


def dot_second(left, right):
    return lax.dot_general(
        left, right, (((1,), (1,)), ((), ())), preferred_element_type=jnp.float32
    )


def split_heads(matrix, seq_count):
    length = matrix.shape[0] // seq_count
    head_count = matrix.shape[1] // HEAD
    shaped = matrix.reshape(seq_count, length, head_count, HEAD)
    return jnp.transpose(shaped, (0, 2, 1, 3)).reshape(seq_count * head_count, length, HEAD)


def join_heads(stacked, seq_count):
    head_count = stacked.shape[0] // seq_count
    length = stacked.shape[1]
    shaped = stacked.reshape(seq_count, head_count, length, HEAD)
    return jnp.transpose(shaped, (0, 2, 1, 3)).reshape(seq_count * length, head_count * HEAD)


def visible_mask(segment_row):
    places = jnp.arange(segment_row.shape[0])
    return (segment_row[:, None] == segment_row[None, :]) & (places[:, None] >= places[None, :])


def attend_forward(operands):
    query_h, key_h, value_h, segment_row, prefix_key, prefix_value = operands
    score_scale = HEAD ** (-0.5)
    score_tok = jnp.where(
        visible_mask(segment_row), dot_second(query_h, key_h) * score_scale, -1e30
    )
    score_pre = dot_second(query_h, prefix_key) * score_scale
    top_score = jnp.maximum(jnp.max(score_tok, axis=1), jnp.max(score_pre, axis=1))[:, None]
    exp_tok = jnp.exp(score_tok - top_score)
    exp_pre = jnp.exp(score_pre - top_score)
    total_mass = jnp.sum(exp_tok, axis=1, keepdims=True) + jnp.sum(exp_pre, axis=1, keepdims=True)
    weight_tok = (exp_tok / total_mass).astype(jnp.bfloat16)
    weight_pre = (exp_pre / total_mass).astype(jnp.bfloat16)
    output_h = dot_plain(weight_tok, value_h) + dot_plain(weight_pre, prefix_value)
    return (output_h, (top_score + jnp.log(total_mass))[:, 0])


def attend_backward(operands):
    query_h, key_h, value_h, segment_row, prefix_key, prefix_value, log_total, grad_h = operands
    score_scale = HEAD ** (-0.5)
    score_tok = jnp.where(
        visible_mask(segment_row), dot_second(query_h, key_h) * score_scale, -1e30
    )
    score_pre = dot_second(query_h, prefix_key) * score_scale
    prob_tok = jnp.exp(score_tok - log_total[:, None])
    prob_pre = jnp.exp(score_pre - log_total[:, None])
    dprob_tok = dot_second(grad_h, value_h)
    dprob_pre = dot_second(grad_h, prefix_value)
    inner_sum = jnp.sum(prob_tok * dprob_tok, axis=1, keepdims=True) + jnp.sum(
        prob_pre * dprob_pre, axis=1, keepdims=True
    )
    dscore_tok = (prob_tok * (dprob_tok - inner_sum)).astype(jnp.bfloat16)
    dscore_pre = (prob_pre * (dprob_pre - inner_sum)).astype(jnp.bfloat16)
    grad_query = (dot_plain(dscore_tok, key_h) + dot_plain(dscore_pre, prefix_key)) * score_scale
    grad_key = dot_first(dscore_tok, query_h) * score_scale
    grad_value = dot_first(prob_tok.astype(jnp.bfloat16), grad_h)
    grad_pkey = dot_first(dscore_pre, query_h) * score_scale
    grad_pvalue = dot_first(prob_pre.astype(jnp.bfloat16), grad_h)
    return (grad_query, grad_key, grad_value, grad_pkey, grad_pvalue)


def adapter_back(prefix_low, prefix_embed, w_mid, w_kv, mid_act):
    grad_kv_w = dot_first(mid_act.astype(jnp.bfloat16), prefix_low)
    grad_kv_b = jnp.sum(prefix_low.astype(jnp.float32), axis=0)
    grad_mid = dot_second(prefix_low, w_kv)
    grad_mid_low = (grad_mid * (1.0 - mid_act * mid_act)).astype(jnp.bfloat16)
    grad_mid_w = dot_first(prefix_embed, grad_mid_low)
    grad_mid_b = jnp.sum(grad_mid_low.astype(jnp.float32), axis=0)
    grad_embed = dot_second(grad_mid_low, w_mid)
    return (grad_embed, grad_mid_w, grad_mid_b, grad_kv_w, grad_kv_b)


def body(
    tokens,
    segments,
    cotangent,
    ln1_gain,
    ln1_bias,
    w_qkv,
    b_qkv,
    w_out,
    b_out,
    ln2_gain,
    ln2_bias,
    w_fc,
    b_fc,
    w_proj,
    b_proj,
    prefix_embed,
    w_mid,
    b_mid,
    w_kv,
    b_kv,
):
    width = tokens.shape[1]
    seq_count = tokens.shape[0] // LENGTH
    head_count = width // HEAD
    gain_one, shift_one, qkv_weight, qkv_bias, out_weight, out_bias = (
        lax.all_gather(ln1_gain, ("dp", "fsdp"), axis=0, tiled=True),
        lax.all_gather(ln1_bias, ("dp", "fsdp"), axis=0, tiled=True),
        lax.all_gather(w_qkv, ("dp", "fsdp"), axis=0, tiled=True),
        lax.all_gather(b_qkv, ("dp", "fsdp"), axis=0, tiled=True),
        lax.all_gather(w_out, ("dp", "fsdp"), axis=0, tiled=True),
        lax.all_gather(b_out, ("dp", "fsdp"), axis=0, tiled=True),
    )
    gain_two, shift_two, fc_weight, fc_bias, proj_weight, proj_bias = (
        lax.all_gather(ln2_gain, ("dp", "fsdp"), axis=0, tiled=True),
        lax.all_gather(ln2_bias, ("dp", "fsdp"), axis=0, tiled=True),
        lax.all_gather(w_fc, ("dp", "fsdp"), axis=0, tiled=True),
        lax.all_gather(b_fc, ("dp", "fsdp"), axis=0, tiled=True),
        lax.all_gather(w_proj, ("dp", "fsdp"), axis=0, tiled=True),
        lax.all_gather(b_proj, ("dp", "fsdp"), axis=0, tiled=True),
    )
    mid_act = jnp.tanh(dot_plain(prefix_embed, w_mid) + b_mid.astype(jnp.float32))
    prefix_kv = (dot_plain(mid_act.astype(jnp.bfloat16), w_kv) + b_kv.astype(jnp.float32)).astype(
        jnp.bfloat16
    )
    prefix_heads = jnp.transpose(prefix_kv.reshape(PREFIX, 2, head_count, HEAD), (1, 2, 0, 3))
    pkey_blocks = jnp.tile(prefix_heads[0], (seq_count, 1, 1))
    pvalue_blocks = jnp.tile(prefix_heads[1], (seq_count, 1, 1))
    segment_blocks = jnp.repeat(segments.reshape(seq_count, LENGTH), head_count, axis=0)
    residual_in = tokens.astype(jnp.float32)
    normed_one = layer_norm(
        residual_in, gain_one.astype(jnp.float32), shift_one.astype(jnp.float32)
    )
    qkv_low = (
        dot_plain(normed_one.astype(jnp.bfloat16), qkv_weight) + qkv_bias.astype(jnp.float32)
    ).astype(jnp.bfloat16)
    query_blocks = split_heads(qkv_low[:, :width], seq_count)
    key_blocks = split_heads(qkv_low[:, width : 2 * width], seq_count)
    value_blocks = split_heads(qkv_low[:, 2 * width :], seq_count)
    hidden_blocks, lse_blocks = lax.map(
        attend_forward,
        (query_blocks, key_blocks, value_blocks, segment_blocks, pkey_blocks, pvalue_blocks),
    )
    hidden_low = join_heads(hidden_blocks, seq_count).astype(jnp.bfloat16)
    mixed = residual_in + dot_plain(hidden_low, out_weight) + out_bias.astype(jnp.float32)
    normed_two = layer_norm(mixed, gain_two.astype(jnp.float32), shift_two.astype(jnp.float32))
    pre_act = dot_plain(normed_two.astype(jnp.bfloat16), fc_weight) + fc_bias.astype(jnp.float32)
    act_low = gelu_tanh(pre_act).astype(jnp.bfloat16)
    block_out = (mixed + dot_plain(act_low, proj_weight) + proj_bias.astype(jnp.float32)).astype(
        jnp.bfloat16
    )
    gain_two_back, fc_back, proj_back = (
        lax.all_gather(ln2_gain, ("dp", "fsdp"), axis=0, tiled=True),
        lax.all_gather(w_fc, ("dp", "fsdp"), axis=0, tiled=True),
        lax.all_gather(w_proj, ("dp", "fsdp"), axis=0, tiled=True),
    )
    grad_act = dot_second(cotangent, proj_back)
    _, gelu_pull = jax.vjp(gelu_tanh, pre_act)
    grad_pre = gelu_pull(grad_act)[0].astype(jnp.bfloat16)
    grad_normed_two = dot_second(grad_pre, fc_back)
    grad_mixed = cotangent.astype(jnp.float32) + norm_back(
        mixed, gain_two_back.astype(jnp.float32), grad_normed_two
    )
    gain_one_back, qkv_back, out_back = (
        lax.all_gather(ln1_gain, ("dp", "fsdp"), axis=0, tiled=True),
        lax.all_gather(w_qkv, ("dp", "fsdp"), axis=0, tiled=True),
        lax.all_gather(w_out, ("dp", "fsdp"), axis=0, tiled=True),
    )
    grad_hidden = dot_second(grad_mixed.astype(jnp.bfloat16), out_back).astype(jnp.bfloat16)
    grad_blocks = split_heads(grad_hidden, seq_count)
    grad_qb, grad_kb, grad_vb, grad_pkb, grad_pvb = lax.map(
        attend_backward,
        (
            query_blocks,
            key_blocks,
            value_blocks,
            segment_blocks,
            pkey_blocks,
            pvalue_blocks,
            lse_blocks,
            grad_blocks,
        ),
    )
    grad_qkv = jnp.concatenate(
        [
            join_heads(grad_qb, seq_count),
            join_heads(grad_kb, seq_count),
            join_heads(grad_vb, seq_count),
        ],
        1,
    ).astype(jnp.bfloat16)
    prefix_grad_key = jnp.transpose(
        jnp.sum(grad_pkb.reshape(seq_count, head_count, PREFIX, HEAD), axis=0), (1, 0, 2)
    ).reshape(PREFIX, width)
    prefix_grad_value = jnp.transpose(
        jnp.sum(grad_pvb.reshape(seq_count, head_count, PREFIX, HEAD), axis=0), (1, 0, 2)
    ).reshape(PREFIX, width)
    grad_prefix = jnp.concatenate([prefix_grad_key, prefix_grad_value], 1)
    total_prefix = lax.psum(grad_prefix, ("dp", "fsdp"))
    grad_embed, grad_mid_w, grad_mid_b, grad_kv_w, grad_kv_b = adapter_back(
        total_prefix.astype(jnp.bfloat16), prefix_embed, w_mid, w_kv, mid_act
    )
    grad_normed_one = dot_second(grad_qkv, qkv_back)
    grad_tokens = (
        grad_mixed + norm_back(residual_in, gain_one_back.astype(jnp.float32), grad_normed_one)
    ).astype(jnp.bfloat16)
    return (block_out, grad_tokens, grad_embed, grad_mid_w, grad_mid_b, grad_kv_w, grad_kv_b)


def solution(mesh):
    return jax.shard_map(
        body,
        mesh=mesh,
        in_specs=(
            P(("dp", "fsdp"), None),
            P(("dp", "fsdp")),
            P(("dp", "fsdp"), None),
            P(("dp", "fsdp")),
            P(("dp", "fsdp")),
            P(("dp", "fsdp"), None),
            P(("dp", "fsdp")),
            P(("dp", "fsdp"), None),
            P(("dp", "fsdp")),
            P(("dp", "fsdp")),
            P(("dp", "fsdp")),
            P(("dp", "fsdp"), None),
            P(("dp", "fsdp")),
            P(("dp", "fsdp"), None),
            P(("dp", "fsdp")),
            P(),
            P(),
            P(),
            P(),
            P(),
        ),
        out_specs=(P(("dp", "fsdp"), None), P(("dp", "fsdp"), None), P(), P(), P(), P(), P()),
        check_vma=False,
    )
```

profile of v0, /device:TPU:0, one launch (start us, length us, event | category | flops | bytes accessed | tf_op | source)
XLA Modules:
  0.0 796.6 jit_solution(311404560958513853)
XLA Ops:
  15.9 42.6 %all-reduce.7 = (bf16[1024]{0:T(1024)(128)(2,1)S(1)}, bf16[3072]{0:T(1024)(128)(2,1)S(1)}, bf16[1024]{0:T(1024)(128)(2,1)S(1)}, bf16[1024]{0:T(1024)(128)(2,1)S(...) all-reduce(bf16[1024]{0:T(1024)(128)(2,1)S(1)} %dynamic-update-slic, ...), channel_id=1, replica_groups=mesh['dp'=8,'fsdp'=4] {'dp','fsdp'}, use_global_device_ids=true, to_apply=%add.3 | all-reduce | flops 9216 | bytes 36864
  58.6 4.2 copy.57
  69.2 65.5 %all-gather = bf16[32,1,128]{2,1,0:T(2,128)(2,1)S(1)} all-gather(bf16[1,1,128]{2,1,0:T(2,128)(2,1)S(1)} %bitcast.258), channel_id=1, replica_groups=mesh['dp'=8,'fsdp'=4] {'dp','fsdp'}, dimensions={0}, use_global_device_ids=true | all-gather | bytes 8448 | tf_op jit(solution)/shard_map/all_gather | solution.py:155
  134.7 4.0 copy.66
  138.7 10.7 %add_convert_fusion = bf16[1024,3072]{1,0:T(8,128)(2,1)S(1)} fusion(f32[3072]{0:T(1024)S(1)} %convert_element_type.119, bf16[1024,3072]{1,0:T(8,128)(2,1)} %all-gather.6.cloned.1.call-done, bf16[1024,1024]{0,1:T(8,128)(2,1)} %copy.57, f32[1024]{0:T(1024)S(1)} %convert_element_type.117, f32[1024]{0:T(1024)S(1)} %convert_element_type.116, ...), kind=kOutput, calls=%fused_computation.114 | convolution fusion | flops 6455033856 | bytes 14708736 | tf_op jit(solution)/shard_map/dot_general | solution.py:32
  152.2 4.0 copy.58
  156.2 4.7 copy.62
  161.0 3.9 copy.59
  164.9 4.8 copy.63
  169.7 3.9 copy.61
  173.7 4.8 copy.64
  180.1 128.1 %while.30 = (s32[]{:T(128)}, bf16[16,1024,64]{1,2,0:T(8,128)(2,1)}, f32[16,1024]{1,0:T(8,128)}, s32[16,1024]{1,0:T(8,128)S(1)}, bf16[16,1024,64]{2,1,0:T(8,128)(...) while((s32[]{:T(128)}, bf16[16,1024,64]{1,2,0:T(8,128)(2,1)}, ...), condition=%wide.region_7.8_spmd, body=%wide.region_2.7_spmd.sunk | while | flops 282727424 | bytes 14675073 | solution.py:177
  308.2 5.7 fusion.154
  316.4 16.8 %fusion.115 = f32[1024,4096]{1,0:T(8,128)} fusion(bf16[1024,4096]{1,0:T(8,128)(2,1)} %all-gather.10.cloned.1.call-done, f32[1024,1024]{0,1:T(8,128)} %copy-done.2, f32[1024]{0:T(1024)S(1)} %convert_element_type.131, f32[1024]{0:T(1024)S(1)} %convert_element_type.130, f32[1024]{0:T(1024)S(1)} %fusion.136, f32[1024]{0:T(1024)S(1)} %broadcast_multiply_fusion), kind=kOutput, calls=%fused_computation.148 | convolution fusion | flops 8595177472 | bytes 29376512 | tf_op jit(solution)/shard_map/dot_general | solution.py:32
  333.1 30.5 %multiply_reduce_fusion.2 = (f32[1024]{0:T(1024)S(1)}, f32[1024,1024]{0,1:T(8,128)}) fusion(f32[1024,1024]{0,1:T(8,128)} %copy-done.2, f32[1024]{0:T(1024)S(1)} %convert_element_type.130, f32[1024]{0:T(1024)S(1)} %broadcast_multiply_fusion, bf16[1024,4096]{1,0:T(8,128)(2,1)} %all-gather.10.cloned.1.call-done, f32[1024,4096]{1,0:T(8,128)} %fusion.115, ...), kind=kOutput, calls=%fused_computation.140 | convolution fusion | flops 17272143872 | bytes 44068864 | tf_op jit(solution)/shard_map/dot_general | solution.py:42
  363.7 4.7 fusion.150
  368.4 3.7 fusion.126
  372.1 4.8 copy.67
  381.7 313.7 %while.31 = (s32[]{:T(128)}, bf16[16,1024,64]{1,2,0:T(8,128)(2,1)}, bf16[16,1024,64]{1,2,0:T(8,128)(2,1)}, bf16[16,1024,64]{1,2,0:T(8,128)(2,1)}, f32[16,10,64]{...) while((s32[]{:T(128)}, bf16[16,1024,64]{1,2,0:T(8,128)(2,1)}, ...), condition=%wide.region_15.16_spmd, body=%wide.region_12.15_spmd.sunk | while | flops 690503296 | bytes 36095136 | solution.py:208
  406.2 3.1 multiply_reduce_fusion.7
  445.4 3.1 multiply_reduce_fusion.7
  504.2 3.1 multiply_reduce_fusion.7
  523.9 3.1 multiply_reduce_fusion.7
  543.5 3.1 multiply_reduce_fusion.7
  582.6 3.1 multiply_reduce_fusion.7
  641.4 3.1 multiply_reduce_fusion.7
  697.5 39.6 %psum.7 = bf16[10,2048]{1,0:T(8,128)(2,1)S(1)} all-reduce(f32[10,2048]{1,0:T(8,128)S(1)} %pad_maximum_fusion), channel_id=1, replica_groups=mesh['dp'=8,'fsdp'=4] {'dp','fsdp'}, use_global_device_ids=true, to_apply=%region_18.19 | all-reduce | flops 20480 | bytes 122880 | tf_op jit(solution)/shard_map/psum | solution.py:236
  744.6 17.1 %add_convert_fusion.2 = bf16[1024,1024]{0,1:T(8,128)(2,1)} fusion(f32[1024,1024]{0,1:T(8,128)} %copy-done.2, f32[1024]{0:T(1024)S(1)} %copy-done.23, bf16[4096,1024]{1,0:T(8,128)(2,1)} %all-gather.12.cloned.1.call-done, f32[1024,4096]{1,0:T(8,128)} %fusion.115, f32[4096]{0:T(1024)S(1)} %bitcast.257), kind=kOutput, calls=%fused_computation.141 | convolution fusion | flops 8635023360 | bytes 31477760 | tf_op jit(solution)/shard_map/dot_general | solution.py:32
  761.7 3.9 copy.73
  765.7 11.2 %fusion.109 = (f32[1024]{0:T(1024)S(1)}, f32[1024,1024]{0,1:T(8,128)S(1)}) fusion(bf16[1024,1024]{0,1:T(8,128)(2,1)} %copy.57, f32[1024]{0:T(1024)S(1)} %copy-done.18, f32[1024]{0:T(1024)S(1)} %copy-done.14, bf16[1024,3072]{1,0:T(8,128)(2,1)} %all-gather.6.cloned.1.call-done, bf16[1024,1024]{0,1:T(8,128)(2,1)} %bitcast.246, ...), kind=kOutput, calls=%fused_computation.136 | convolution fusion | flops 6466567168 | bytes 18886656 | tf_op jit(solution)/shard_map/dot_general | solution.py:42
  779.7 3.3 add_convert_fusion.1
  783.0 3.9 copy.74
  (520 shorter events, 460.4 us)
Async XLA Ops:
  7.2 60.8 %copy-start = (bf16[512,2048]{1,0:T(8,128)(2,1)S(1)}, bf16[512,2048]{1,0:T(8,128)(2,1)}, u32[]{:S(2)}) copy-start(bf16[512,2048]{1,0:T(8,128)(2,1)} %param.42) | copy-start | bytes 6291460
  7.2 131.5 %all-gather.6.cloned.1.call-start = ((), (), s32[]{:S(2)}) async-start(), calls=%async_computation | async-start | bytes 6488064 | tf_op jit(solution)/shard_map/all_gather | solution.py:146
  7.9 300.3 %all-gather.8.cloned.1.call-start = ((), (), s32[]{:S(2)}) async-start(), calls=%async_computation.1 | async-start | bytes 2162688 | tf_op jit(solution)/shard_map/all_gather | solution.py:148
  8.7 307.7 %all-gather.10.cloned.1.call-start = ((), (), s32[]{:S(2)}) async-start(), calls=%async_computation.2 | async-start | bytes 8650752 | tf_op jit(solution)/shard_map/all_gather | solution.py:154
  9.4 323.8 %all-gather.12.cloned.1.call-start = ((), (), s32[]{:S(2)}) async-start(), calls=%async_computation.3 | async-start | bytes 8650752 | tf_op jit(solution)/shard_map/all_gather | solution.py:156
  58.5 8.5 %copy-start.21 = (bf16[2048]{0:T(1024)(128)(2,1)S(1)}, bf16[2048]{0:T(1024)(128)(2,1)}, u32[]{:S(2)}) copy-start(bf16[2048]{0:T(1024)(128)(2,1)} %param.43) | copy-start | bytes 12292
  58.5 8.5 %copy-start.24 = (bf16[512]{0:T(512)(128)(2,1)S(1)}, bf16[512]{0:T(512)(128)(2,1)}, u32[]{:S(2)}) copy-start(bf16[512]{0:T(512)(128)(2,1)} %param.41) | copy-start | bytes 3076
  58.5 8.5 %copy-start.7 = (bf16[1024,512]{1,0:T(8,128)(2,1)S(1)}, bf16[1024,512]{1,0:T(8,128)(2,1)}, u32[]{:S(2)}) copy-start(bf16[1024,512]{1,0:T(8,128)(2,1)} %param.40) | copy-start | bytes 3145732
  58.5 8.5 %copy-start.11 = (bf16[10,1024]{1,0:T(8,128)(2,1)S(1)}, bf16[10,1024]{1,0:T(8,128)(2,1)}, u32[]{:S(2)}) copy-start(bf16[10,1024]{1,0:T(8,128)(2,1)} %param.39) | copy-start | bytes 61444
  62.8 6.4 copy-start.25
  62.8 75.9 %copy-start.17 = (f32[1024]{0:T(1024)}, f32[1024]{0:T(1024)S(1)}, u32[]{:S(2)}) copy-start(f32[1024]{0:T(1024)S(1)} %convert_element_type.116) | copy-start | bytes 12292
  64.8 73.9 %copy-start.13 = (f32[1024]{0:T(1024)}, f32[1024]{0:T(1024)S(1)}, u32[]{:S(2)}) copy-start(f32[1024]{0:T(1024)S(1)} %broadcast_multiply_fusion.1) | copy-start | bytes 12292
  67.0 82.4 %copy-start.15 = (f32[1024]{0:T(1024)}, f32[1024]{0:T(1024)S(1)}, u32[]{:S(2)}) copy-start(f32[1024]{0:T(1024)S(1)} %fusion.105) | copy-start | bytes 12292
  67.0 82.3 %copy-start.19 = (f32[1024]{0:T(1024)}, f32[1024]{0:T(1024)S(1)}, u32[]{:S(2)}) copy-start(f32[1024]{0:T(1024)S(1)} %fusion.135) | copy-start | bytes 12292
  67.3 0.6 copy-start.9
  173.7 4.8 copy-start.22
  313.9 2.0 copy-start.2
  363.6 4.7 copy-start.5
  363.7 4.7 copy-start.26
  368.3 3.7 copy-start.3
  381.7 355.4 %copy-start.10 = (f32[10,512]{1,0:T(8,128)S(1)}, f32[10,512]{1,0:T(8,128)}, u32[]{:S(2)}) copy-start(f32[10,512]{1,0:T(8,128)} %copy-done.9) | copy-start | bytes 61444
  381.7 356.7 %copy-start.8 = (bf16[1024,512]{1,0:T(8,128)(2,1)S(1)}, bf16[1024,512]{1,0:T(8,128)(2,1)}, u32[]{:S(2)}) copy-start(bf16[1024,512]{1,0:T(8,128)(2,1)} %param.40) | copy-start | bytes 3145732
  695.4 44.0 %copy-start.12 = (bf16[10,1024]{1,0:T(8,128)(2,1)S(1)}, bf16[10,1024]{1,0:T(8,128)(2,1)}, u32[]{:S(2)}) copy-start(bf16[10,1024]{1,0:T(8,128)(2,1)} %param.39) | copy-start | bytes 61444
  738.4 6.2 copy-start.23
  761.7 3.9 copy-start.14
  761.7 3.9 copy-start.18
  765.7 11.2 %copy-start.16 = (f32[1024]{0:T(1024)S(1)}, f32[1024]{0:T(1024)}, u32[]{:S(2)}) copy-start(f32[1024]{0:T(1024)} %copy-done.15) | copy-start | bytes 12292
  765.7 11.3 %copy-start.1 = (bf16[1024,1024]{0,1:T(8,128)(2,1)S(1)}, bf16[1024,1024]{0,1:T(8,128)(2,1)}, u32[]{:S(2)}) copy-start(bf16[1024,1024]{0,1:T(8,128)(2,1)} %copy.57) | copy-start | bytes 6291460
  765.7 11.3 %copy-start.20 = (f32[1024]{0:T(1024)S(1)}, f32[1024]{0:T(1024)}, u32[]{:S(2)}) copy-start(f32[1024]{0:T(1024)} %copy-done.19) | copy-start | bytes 12292
  776.9 2.2 copy-start.4
  776.9 2.9 copy-start.6
Sparse Core Ops, SparseCore 0:
  10.9 72.6 all-gather.5
  86.5 54.9 all-gather.7
  144.4 76.2 all-gather.9
  223.6 75.9 all-gather.11
where the time goes:
time: 809 us; the launch traced here: 797 us
  matrix products  479 us (59%)
  blocking collectives  148 us (18%)
  local copies, waits for them, and re-layouts  107 us (13%)
  other arithmetic  44.2 us (5%)
  between operations  14.4 us (2%)
    dot_general x101, matrix products, dot_second(): lax.dot_general(left, right, (((1,), (1,)), ((), ())), preferred_element_...  211 us
    dot_general x66, matrix products, dot_first(): lax.dot_general(left, right, (((0,), (0,)), ((), ())), preferred_element_...  135 us
    dot_general x70, matrix products, dot_plain(): return jnp.dot(left, right, preferred_element_type=jnp.float32)  132 us
    all_gather x1, blocking collectives, body(): lax.all_gather(b_fc, ('dp', 'fsdp'), axis=0, tiled=True)  65.5 us
    unnamed x1, blocking collectives  42.6 us
    psum x1, blocking collectives, body(): total_prefix = lax.psum(grad_prefix, ('dp', 'fsdp'))  39.6 us
    unnamed x73, local copies, waits for them, and re-layouts  29.1 us
    dynamic_update_slice x16, local copies, waits for them, and re-layouts, body(): lax.map(attend_forward, (query_blocks, key_blocks, value_blocks, segment_...  22.2 us
  transfers between devices with their start and end apart: 4, of which 0 were waited for; matrix products, arithmetic and copies ran while one was open for 27% of the time, Pallas kernels for 0%

commit v1 on v0

v1 whole, which is shorter than its diff:
```python
import jax
import jax.numpy as jnp
from jax import lax
from jax.experimental import pallas as pl
from jax.experimental.pallas import tpu as pltpu
from jax.sharding import PartitionSpec as P

HEAD=64; PREFIX=10; LENGTH=1024; PADP=16
LOG2E=1.4426950408889634
NEG=-1e30
KX=1152
NT=(((1,),(1,)),((),()))
NN=(((1,),(0,)),((),()))
TN=(((0,),(0,)),((),()))
def dg(a,b,d): return lax.dot_general(a,b,d,preferred_element_type=jnp.float32)
SCALE=HEAD**-0.5
C=SCALE*LOG2E

def split3(x):
    hi=x.astype(jnp.bfloat16); r=x-hi.astype(jnp.float32)
    mid=r.astype(jnp.bfloat16); r=r-mid.astype(jnp.float32)
    return hi.astype(jnp.float32),mid.astype(jnp.float32),r

QB=((0,240,256),(240,496,512),(496,752,768),(752,1024,1152))
def fwd_kernel(sc_ref, sr_ref, q_ref, k_ref, v_ref, pk_ref, pv_ref, o_ref, l_ref, bias, kx, vx):
    @pl.when(pl.program_id(0)==0)
    def _():
        row=lax.broadcasted_iota(jnp.int32,(LENGTH,KX),0)+PADP
        col=lax.broadcasted_iota(jnp.int32,(LENGTH,KX),1)
        ok=((sc_ref[...]==sr_ref[...])&(col<=row))|(col<PREFIX)
        bias[...]=jnp.where(ok,0.0,NEG)
        kx[...]=jnp.zeros_like(kx); vx[...]=jnp.zeros_like(vx)
    lane=lax.broadcasted_iota(jnp.int32,(1,128),1)
    for h in range(2):
        mh=((lane>=64*h)&(lane<64*h+64))
        z=jnp.bfloat16(0)
        kx[h,:PADP,:]=jnp.where(mh,pk_ref[...],z); kx[h,PADP:PADP+LENGTH,:]=jnp.where(mh,k_ref[...],z)
        vx[h,:PADP,:128]=jnp.where(mh,pv_ref[...],z); vx[h,PADP:PADP+LENGTH,:128]=jnp.where(mh,v_ref[...],z)
        vx[h,:,128:]=jnp.ones((KX,128),jnp.bfloat16)
    for a,b,nk in QB:
        outs=[]; ls=[]
        for h in range(2):
            s=dg(q_ref[a:b,:],kx[h,:nk,:],NT)
            s=s*C+bias[a:b,:nk]
            m=jnp.max(s,axis=1,keepdims=True)
            p=jnp.exp2(s-m).astype(jnp.bfloat16)
            o=dg(p,vx[h,:nk,:],NN)
            l=o[:,128:]
            outs.append(o[:,:128]/l)
            ls.append(-(m+jnp.log2(l))*(1.0/C))
        o_ref[a:b,:]=(outs[0]+outs[1]).astype(jnp.bfloat16)
        h0,m0,l0=split3(ls[0]); h1,m1,l1=split3(ls[1])
        aug=jnp.where(lane==0,h0,jnp.where(lane==1,m0,jnp.where(lane==2,l0,jnp.where(lane==3,h1,jnp.where(lane==4,m1,jnp.where(lane==5,l1,0.0))))))
        l_ref[a:b,:]=aug.astype(jnp.bfloat16)

def attn_fwd(qkv, prefix_kv16, seg):
    D=qkv.shape[1]//3; nh=D//128
    sc=seg[:,None]
    sr=jnp.concatenate([jnp.full((PADP,),-1,jnp.int32),seg,jnp.full((KX-PADP-LENGTH,),-1,jnp.int32)])[None,:]
    return pl.pallas_call(fwd_kernel,grid=(nh,),
      in_specs=[pl.BlockSpec((LENGTH,1),lambda h:(0,0)),pl.BlockSpec((1,KX),lambda h:(0,0)),
        pl.BlockSpec((LENGTH,128),lambda h:(0,h)),pl.BlockSpec((LENGTH,128),lambda h:(0,nh+h)),pl.BlockSpec((LENGTH,128),lambda h:(0,2*nh+h)),
        pl.BlockSpec((PADP,128),lambda h:(0,h)),pl.BlockSpec((PADP,128),lambda h:(0,nh+h))],
      out_specs=[pl.BlockSpec((LENGTH,128),lambda h:(0,h)),pl.BlockSpec((LENGTH,128),lambda h:(0,h))],
      out_shape=[jax.ShapeDtypeStruct((LENGTH,D),jnp.bfloat16),jax.ShapeDtypeStruct((LENGTH,D),jnp.bfloat16)],
      scratch_shapes=[pltpu.VMEM((LENGTH,KX),jnp.float32),pltpu.VMEM((2,KX,128),jnp.bfloat16),pltpu.VMEM((2,KX,256),jnp.bfloat16)],
      compiler_params=pltpu.CompilerParams(vmem_limit_bytes=48*1024*1024),
      cost_estimate=pl.CostEstimate(flops=4*1024*1024*1024,bytes_accessed=10*1024*1024,transcendentals=10*1024*1024),
    )(sc,sr,qkv,qkv,qkv,prefix_kv16,prefix_kv16)

KB=((0,272,0),(272,528,256),(528,784,512),(784,1040,768))
KY=1040
def make_bwd(variant):
  def bwd_kernel(sc_ref, sr_ref, q_ref, k_ref, v_ref, pk_ref, pv_ref, l_ref, o_ref, g_ref,
                 dq_ref, dk_ref, dv_ref, dpk_ref, dpv_ref, bias, qa, ga, ka, va, dq):
    @pl.when(pl.program_id(0)==0)
    def _():
        row=lax.broadcasted_iota(jnp.int32,(KY,LENGTH),0)
        col=lax.broadcasted_iota(jnp.int32,(KY,LENGTH),1)+PADP
        ok=((sc_ref[...]==sr_ref[...])&(row<=col))|(row<PREFIX)
        bias[...]=jnp.where(ok,0.0,NEG)
    lane=lax.broadcasted_iota(jnp.int32,(1,128),1)
    z=jnp.bfloat16(0)
    qa[:,:128]=q_ref[...]; qa[:,128:]=l_ref[...]
    ga[:,:128]=g_ref[...]
    prod=g_ref[...].astype(jnp.float32)*o_ref[...].astype(jnp.float32)
    aug=None
    for h in range(2):
        mh=((lane>=64*h)&(lane<64*h+64))
        d=-jnp.sum(jnp.where(mh,prod,0.0),axis=1,keepdims=True)
        hi,mid,lo=split3(d)
        t=jnp.where(lane==3*h,hi,jnp.where(lane==3*h+1,mid,jnp.where(lane==3*h+2,lo,0.0)))
        aug=t if aug is None else aug+t
        one=jnp.where((lane>=3*h)&(lane<3*h+3),1.0,0.0).astype(jnp.bfloat16)
        ka[h,:PADP,:128]=jnp.where(mh,pk_ref[...],z); ka[h,PADP:,:128]=jnp.where(mh,k_ref[...],z)
        va[h,:PADP,:128]=jnp.where(mh,pv_ref[...],z); va[h,PADP:,:128]=jnp.where(mh,v_ref[...],z)
        ka[h,:,128:]=jnp.broadcast_to(one,(KY,128)); va[h,:,128:]=jnp.broadcast_to(one,(KY,128))
    ga[:,128:]=aug.astype(jnp.bfloat16)
    for i,(a,b,q0) in enumerate(KB):
        dk=None; dv=None; dqs=[]
        for h in range(2):
            mh=((lane>=64*h)&(lane<64*h+64))
            s=dg(ka[h,a:b,:],qa[q0:,:],NT)
            p=jnp.exp2(s*C+bias[a:b,q0:])
            dp=dg(va[h,a:b,:],ga[q0:,:],NT)
            ds=(p*dp).astype(jnp.bfloat16)
            pb=p.astype(jnp.bfloat16)
            tv=dg(pb,jnp.where(mh,g_ref[q0:,:],z),NN)
            tk=dg(ds,jnp.where(mh,q_ref[q0:,:],z),NN)
            dv=tv if dv is None else dv+tv
            dk=tk if dk is None else dk+tk
            if variant=="tn":
                dqs.append(dg(ds,ka[h,a:b,:128],TN))
            else:
                kt=ka[h,a:b,:128].T
                dqs.append(dg(kt,ds,NN))
        t=dqs[0]+dqs[1]
        if variant=="tn":
            if i==0: dq[...]=t
            else: dq[q0:,:]+=t
        else:
            if i==0: dq[...]=t
            else: dq[:,q0:]+=t
        if i==0:
            dpk_ref[...]=dk[:PADP]*SCALE; dpv_ref[...]=dv[:PADP]
            dk_ref[:256,:]=(dk[PADP:]*SCALE).astype(jnp.bfloat16); dv_ref[:256,:]=dv[PADP:].astype(jnp.bfloat16)
        else:
            dk_ref[q0:q0+256,:]=(dk*SCALE).astype(jnp.bfloat16); dv_ref[q0:q0+256,:]=dv.astype(jnp.bfloat16)
    r=dq[...] if variant=="tn" else dq[...].T
    dq_ref[...]=(r*SCALE).astype(jnp.bfloat16)
  return bwd_kernel

def attn_bwd(qkv, prefix_kv16, seg, lse, o, g, variant="tn"):
    D=qkv.shape[1]//3; nh=D//128
    sr=seg[None,:]
    sc=jnp.concatenate([jnp.full((PADP,),-1,jnp.int32),seg])[:,None]
    blk=lambda off: pl.BlockSpec((LENGTH,128),lambda h,off=off:(0,off+h))
    pblk=lambda off: pl.BlockSpec((PADP,128),lambda h,off=off:(0,off+h))
    return pl.pallas_call(make_bwd(variant),grid=(nh,),
      in_specs=[pl.BlockSpec((KY,1),lambda h:(0,0)),pl.BlockSpec((1,LENGTH),lambda h:(0,0)),
        blk(0),blk(nh),blk(2*nh),pblk(0),pblk(nh),blk(0),blk(0),blk(0)],
      out_specs=[blk(0)]*3+[pblk(0)]*2,
      out_shape=[jax.ShapeDtypeStruct((LENGTH,D),jnp.bfloat16)]*3+[jax.ShapeDtypeStruct((PADP,D),jnp.float32)]*2,
      scratch_shapes=[pltpu.VMEM((KY,LENGTH),jnp.float32),pltpu.VMEM((LENGTH,256),jnp.bfloat16),pltpu.VMEM((LENGTH,256),jnp.bfloat16),
         pltpu.VMEM((2,KY,256),jnp.bfloat16),pltpu.VMEM((2,KY,256),jnp.bfloat16),
         pltpu.VMEM((LENGTH,128) if variant=="tn" else (128,LENGTH),jnp.float32)],
      compiler_params=pltpu.CompilerParams(vmem_limit_bytes=56*1024*1024),
      cost_estimate=pl.CostEstimate(flops=10*1024*1024*1024,bytes_accessed=16*1024*1024,transcendentals=10*1024*1024),
    )(sc,sr,qkv,qkv,qkv,prefix_kv16,prefix_kv16,lse,o,g)


def layer_norm(values, gain_row, shift_row):
    row_mean = jnp.mean(values, axis=-1, keepdims=True)
    centred = values - row_mean
    spread = jnp.mean(centred * centred, axis=-1, keepdims=True)
    return centred * lax.rsqrt(spread + 1e-05) * gain_row + shift_row


def norm_back(values, gain_row, grad_in):

    def apply_norm(inner_values):
        return layer_norm(inner_values, gain_row, 0.0)

    _, pullback = jax.vjp(apply_norm, values)
    return pullback(grad_in)[0]


def gelu_tanh(values):
    return jax.nn.gelu(values, approximate=True)


def dot_plain(left, right):
    return jnp.dot(left, right, preferred_element_type=jnp.float32)


def dot_first(left, right):
    return lax.dot_general(
        left, right, (((0,), (0,)), ((), ())), preferred_element_type=jnp.float32
    )


def dot_second(left, right):
    return lax.dot_general(
        left, right, (((1,), (1,)), ((), ())), preferred_element_type=jnp.float32
    )


def adapter_back(prefix_low, prefix_embed, w_mid, w_kv, mid_act):
    grad_kv_w = dot_first(mid_act.astype(jnp.bfloat16), prefix_low)
    grad_kv_b = jnp.sum(prefix_low.astype(jnp.float32), axis=0)
    grad_mid = dot_second(prefix_low, w_kv)
    grad_mid_low = (grad_mid * (1.0 - mid_act * mid_act)).astype(jnp.bfloat16)
    grad_mid_w = dot_first(prefix_embed, grad_mid_low)
    grad_mid_b = jnp.sum(grad_mid_low.astype(jnp.float32), axis=0)
    grad_embed = dot_second(grad_mid_low, w_mid)
    return (grad_embed, grad_mid_w, grad_mid_b, grad_kv_w, grad_kv_b)


def body(
    tokens,
    segments,
    cotangent,
    ln1_gain,
    ln1_bias,
    w_qkv,
    b_qkv,
    w_out,
    b_out,
    ln2_gain,
    ln2_bias,
    w_fc,
    b_fc,
    w_proj,
    b_proj,
    prefix_embed,
    w_mid,
    b_mid,
    w_kv,
    b_kv,
):
    gain_one, shift_one, qkv_weight, qkv_bias, out_weight, out_bias = (
        lax.all_gather(ln1_gain, ("dp", "fsdp"), axis=0, tiled=True),
        lax.all_gather(ln1_bias, ("dp", "fsdp"), axis=0, tiled=True),
        lax.all_gather(w_qkv, ("dp", "fsdp"), axis=0, tiled=True),
        lax.all_gather(b_qkv, ("dp", "fsdp"), axis=0, tiled=True),
        lax.all_gather(w_out, ("dp", "fsdp"), axis=0, tiled=True),
        lax.all_gather(b_out, ("dp", "fsdp"), axis=0, tiled=True),
    )
    gain_two, shift_two, fc_weight, fc_bias, proj_weight, proj_bias = (
        lax.all_gather(ln2_gain, ("dp", "fsdp"), axis=0, tiled=True),
        lax.all_gather(ln2_bias, ("dp", "fsdp"), axis=0, tiled=True),
        lax.all_gather(w_fc, ("dp", "fsdp"), axis=0, tiled=True),
        lax.all_gather(b_fc, ("dp", "fsdp"), axis=0, tiled=True),
        lax.all_gather(w_proj, ("dp", "fsdp"), axis=0, tiled=True),
        lax.all_gather(b_proj, ("dp", "fsdp"), axis=0, tiled=True),
    )
    mid_act = jnp.tanh(dot_plain(prefix_embed, w_mid) + b_mid.astype(jnp.float32))
    prefix_kv = (dot_plain(mid_act.astype(jnp.bfloat16), w_kv) + b_kv.astype(jnp.float32)).astype(
        jnp.bfloat16
    )
    prefix_pad = jnp.pad(prefix_kv, ((0, PADP - PREFIX), (0, 0)))
    residual_in = tokens.astype(jnp.float32)
    normed_one = layer_norm(
        residual_in, gain_one.astype(jnp.float32), shift_one.astype(jnp.float32)
    )
    qkv_low = (
        dot_plain(normed_one.astype(jnp.bfloat16), qkv_weight) + qkv_bias.astype(jnp.float32)
    ).astype(jnp.bfloat16)
    hidden_low, lse_aug = attn_fwd(qkv_low, prefix_pad, segments)
    mixed = residual_in + dot_plain(hidden_low, out_weight) + out_bias.astype(jnp.float32)
    normed_two = layer_norm(mixed, gain_two.astype(jnp.float32), shift_two.astype(jnp.float32))
    pre_act = dot_plain(normed_two.astype(jnp.bfloat16), fc_weight) + fc_bias.astype(jnp.float32)
    act_low = gelu_tanh(pre_act).astype(jnp.bfloat16)
    block_out = (mixed + dot_plain(act_low, proj_weight) + proj_bias.astype(jnp.float32)).astype(
        jnp.bfloat16
    )
    gain_two_back, fc_back, proj_back = (
        lax.all_gather(ln2_gain, ("dp", "fsdp"), axis=0, tiled=True),
        lax.all_gather(w_fc, ("dp", "fsdp"), axis=0, tiled=True),
        lax.all_gather(w_proj, ("dp", "fsdp"), axis=0, tiled=True),
    )
    grad_act = dot_second(cotangent, proj_back)
    _, gelu_pull = jax.vjp(gelu_tanh, pre_act)
    grad_pre = gelu_pull(grad_act)[0].astype(jnp.bfloat16)
    grad_normed_two = dot_second(grad_pre, fc_back)
    grad_mixed = cotangent.astype(jnp.float32) + norm_back(
        mixed, gain_two_back.astype(jnp.float32), grad_normed_two
    )
    gain_one_back, qkv_back, out_back = (
        lax.all_gather(ln1_gain, ("dp", "fsdp"), axis=0, tiled=True),
        lax.all_gather(w_qkv, ("dp", "fsdp"), axis=0, tiled=True),
        lax.all_gather(w_out, ("dp", "fsdp"), axis=0, tiled=True),
    )
    grad_hidden = dot_second(grad_mixed.astype(jnp.bfloat16), out_back).astype(jnp.bfloat16)
    gq, gk, gv, gpk, gpv = attn_bwd(qkv_low, prefix_pad, segments, lse_aug, hidden_low, grad_hidden, "kt")
    grad_qkv = jnp.concatenate([gq, gk, gv], 1)
    grad_prefix = jnp.concatenate([gpk[:PREFIX], gpv[:PREFIX]], 1)
    total_prefix = lax.psum(grad_prefix, ("dp", "fsdp"))
    grad_embed, grad_mid_w, grad_mid_b, grad_kv_w, grad_kv_b = adapter_back(
        total_prefix.astype(jnp.bfloat16), prefix_embed, w_mid, w_kv, mid_act
    )
    grad_normed_one = dot_second(grad_qkv, qkv_back)
    grad_tokens = (
        grad_mixed + norm_back(residual_in, gain_one_back.astype(jnp.float32), grad_normed_one)
    ).astype(jnp.bfloat16)
    return (block_out, grad_tokens, grad_embed, grad_mid_w, grad_mid_b, grad_kv_w, grad_kv_b)


def solution(mesh):
    return jax.shard_map(
        body,
        mesh=mesh,
        in_specs=(
            P(("dp", "fsdp"), None),
            P(("dp", "fsdp")),
            P(("dp", "fsdp"), None),
            P(("dp", "fsdp")),
            P(("dp", "fsdp")),
            P(("dp", "fsdp"), None),
            P(("dp", "fsdp")),
            P(("dp", "fsdp"), None),
            P(("dp", "fsdp")),
            P(("dp", "fsdp")),
            P(("dp", "fsdp")),
            P(("dp", "fsdp"), None),
            P(("dp", "fsdp")),
            P(("dp", "fsdp"), None),
            P(("dp", "fsdp")),
            P(),
            P(),
            P(),
            P(),
            P(),
        ),
        out_specs=(P(("dp", "fsdp"), None), P(("dp", "fsdp"), None), P(), P(), P(), P(), P()),
        check_vma=False,
    )
```

time: 809 us -> 483 us (0.60); the launches traced: 797 us -> 479 us
  matrix products: 479 us -> 106 us
  waiting for transfers between devices: 2.62 us -> 95.8 us
  local copies, waits for them, and re-layouts: 107 us -> 33 us
  Pallas kernels: 0 us -> 68.3 us
  other arithmetic: 44.2 us -> 12.9 us
    dot_general x101 -> x5, matrix products: 211 us -> 47.9 us  [dot_second(): lax.dot_general(left, right, (((1,), (1,)), ((), ())), preferred_element_...]
    dot_general x66 -> x2, matrix products: 135 us -> 4.53 us  [dot_first(): lax.dot_general(left, right, (((0,), (0,)), ((), ())), preferred_element_...]
    dot_general x70 -> x6, matrix products: 132 us -> 54.1 us  [dot_plain(): return jnp.dot(left, right, preferred_element_type=jnp.float32)]
    pallas_call x0 -> x2, Pallas kernels: none -> 68.3 us  [the longest x1 39.8 us: attn_bwd(): pl.pallas_call(make_bwd(variant), grid=(nh,), in_specs=[pl.BlockSpec((KY,...]
    all_gather x1, waiting for transfers between devices: 0.01 us -> 62.1 us  [body(): lax.all_gather(w_proj, ('dp', 'fsdp'), axis=0, tiled=True)]
    all_gather x1, waiting for transfers between devices: 0.02 us -> 31.1 us  [body(): lax.all_gather(w_fc, ('dp', 'fsdp'), axis=0, tiled=True)]
    dynamic_update_slice x16 -> x0, local copies, waits for them, and re-layouts: 22.2 us -> none  [body(): lax.map(attend_forward, (query_blocks, key_blocks, value_blocks, segment_...]
    convert_element_type x32 -> x0, other arithmetic: 18.4 us -> none  [the longest x16 18.2 us: attend_backward(): dscore_tok = (prob_tok * (dprob_tok - inner_sum)).astype(jnp.bfloat16)]
  transfers between devices with their start and end apart: 4 -> 4, of which waited for: 0 -> 2; matrix products, arithmetic and copies ran while one was open for 27% -> 11% of each run, Pallas kernels for 0% -> 6%
where the time goes in v1:
time: 483 us; the launch traced here: 479 us
  blocking collectives  149 us (31%)
  matrix products  106 us (22%)
  waiting for transfers between devices  95.8 us (20%)
  Pallas kernels  68.3 us (14%)
  local copies, waits for them, and re-layouts  33 us (7%)
  between operations  14.4 us (3%)
  other arithmetic  12.9 us (3%)
    all_gather x1, blocking collectives, body(): lax.all_gather(b_fc, ('dp', 'fsdp'), axis=0, tiled=True)  65.8 us
    all_gather x1, waiting for transfers between devices, body(): lax.all_gather(w_proj, ('dp', 'fsdp'), axis=0, tiled=True)  62.1 us
    dot_general x6, matrix products, dot_plain(): return jnp.dot(left, right, preferred_element_type=jnp.float32)  54.1 us
    dot_general x5, matrix products, dot_second(): lax.dot_general(left, right, (((1,), (1,)), ((), ())), preferred_element_...  47.9 us
    unnamed x1, blocking collectives  42.6 us
    psum x1, blocking collectives, body(): total_prefix = lax.psum(grad_prefix, ('dp', 'fsdp'))  40.2 us
    pallas_call x1, Pallas kernels, attn_bwd(): pl.pallas_call(make_bwd(variant), grid=(nh,), in_specs=[pl.BlockSpec((KY,...  39.8 us
    unnamed x61, local copies, waits for them, and re-layouts  31.6 us
  transfers between devices with their start and end apart: 4, of which 2 were waited for; matrix products, arithmetic and copies ran while one was open for 11% of the time, Pallas kernels for 6%

profile of v1, /device:TPU:0, one launch (start us, length us, event | category | flops | bytes accessed | tf_op | source)
XLA Modules:
  0.0 479.5 jit_solution(10638851188264036494)
XLA Ops:
  15.9 42.6 %all-reduce.9 = (bf16[1024]{0:T(1024)(128)(2,1)S(1)}, bf16[3072]{0:T(1024)(128)(2,1)S(1)}, bf16[1024]{0:T(1024)(128)(2,1)S(1)}, bf16[1024]{0:T(1024)(128)(2,1)S(...) all-reduce(bf16[1024]{0:T(1024)(128)(2,1)S(1)} %dynamic-update-slic, ...), channel_id=1, replica_groups=mesh['dp'=8,'fsdp'=4] {'dp','fsdp'}, use_global_device_ids=true, to_apply=%add.5 | all-reduce | flops 9216 | bytes 36864
  58.5 4.1 copy.41
  63.1 65.8 %all-gather = bf16[32,1,128]{2,1,0:T(2,128)(2,1)S(1)} all-gather(bf16[1,1,128]{2,1,0:T(2,128)(2,1)S(1)} %bitcast.34), channel_id=1, replica_groups=mesh['dp'=8,'fsdp'=4] {'dp','fsdp'}, dimensions={0}, use_global_device_ids=true | all-gather | bytes 8448 | tf_op jit(solution)/shard_map/all_gather | solution.py:233
  128.9 3.9 copy.44
  132.9 1.0 broadcast_in_dim.27.sc_ref
  134.5 1.5 fusion.44
  138.0 12.3 %add_convert_fusion.q_ref.k_ref.v_ref = bf16[1024,3072]{1,0:T(8,128)(2,1)} fusion(f32[3072]{0:T(1024)S(1)} %convert_element_type.90, bf16[1024,3072]{1,0:T(8,128)(2,1)} %all-gather.6.cloned.1.call-done, bf16[1024,1024]{0,1:T(8,128)(2,1)} %copy.41, f32[1024]{0:T(1024)S(1)} %convert_element_type.88, f32[1024]{0:T(1024)S(1)} %convert_element_type.87, ...), kind=kOutput, calls=%fused_computation.10 | convolution fusion | flops 6455033856 | bytes 14708736 | tf_op jit(solution)/shard_map/dot_general | solution.py:173
  150.3 28.5 %shard_map.243 = (bf16[1024,1024]{1,0:T(8,128)(2,1)S(1)}, bf16[1024,1024]{1,0:T(8,128)(2,1)S(1)}) custom-call(s32[1024,1]{1,0:T(8,128)S(1)} %copy.42.sc_ref, s32[1,1152]{1,0:T(1,128)S(1)} %broadcast_in_dim.20.sr_ref, bf16[1024,3072]{1,0:T(8,128)(2,1)} %add_convert_fusion.q_ref.k_ref.v_ref, bf16[1024,3072]{1,0:T(8,128)(2,1)} %add_convert_fusion.q_ref.k_ref.v_ref, ...), custom_call_target="tpu_custom_call" | custom-call | flops 4294967296 | bytes 10485760 | tf_op jit(solution)/shard_map/pallas_call | solution.py:60
  178.8 1.3 copy-done.2
  180.1 1.3 copy-done.3
  181.5 5.7 %fusion.66 = (f32[1024]{0:T(1024)S(1)}, f32[1024,1024]{0,1:T(8,128)S(1)}) fusion(f32[1024]{0:T(1024)S(1)} %convert_element_type.96, bf16[1024,1024]{1,0:T(8,128)(2,1)} %copy-done.2, bf16[1024,1024]{1,0:T(8,128)(2,1)} %all-gather.8.cloned.1.call-done, bf16[1024,1024]{0,1:T(8,128)(2,1)} %copy.41), kind=kOutput, calls=%fused_computation.91 | convolution fusion | flops 2151676928 | bytes 10493952 | tf_op jit(solution)/shard_map/dot_general | solution.py:173
  187.2 1.9 copy-done.6
  189.6 31.1 %all-gather.10.cloned.1.call-done = bf16[1024,4096]{1,0:T(8,128)(2,1)} async-done(((bf16[32,4096]{1,0:T(8,128)(2,1)}), bf16[1024,4096]{1,0:T(8,128)(2,1)}) %all-gather.10.cloned.1.call-update) | async-done | bytes 8388624 | tf_op jit(solution)/shard_map/all_gather | solution.py:232
  220.7 16.7 %fusion.30 = f32[1024,4096]{1,0:T(8,128)} fusion(bf16[1024,4096]{1,0:T(8,128)(2,1)} %all-gather.10.cloned.1.call-done, f32[1024,1024]{0,1:T(8,128)} %copy-done.6, f32[1024]{0:T(1024)S(1)} %convert_element_type.98, f32[1024]{0:T(1024)S(1)} %convert_element_type.97, f32[1024]{0:T(1024)S(1)} %fusion.51, f32[1024]{0:T(1024)S(1)} %broadcast_multiply_fusion), kind=kOutput, calls=%fused_computation.44 | convolution fusion | flops 8595177472 | bytes 29376512 | tf_op jit(solution)/shard_map/dot_general | solution.py:173
  237.4 62.1 %all-gather.12.cloned.1.call-done = bf16[4096,1024]{1,0:T(8,128)(2,1)} async-done(((bf16[128,1024]{1,0:T(8,128)(2,1)}), bf16[4096,1024]{1,0:T(8,128)(2,1)}) %all-gather.12.cloned.1.call-update) | async-done | bytes 8388624 | tf_op jit(solution)/shard_map/all_gather | solution.py:234
  299.5 30.6 %multiply_reduce_fusion = (f32[1024]{0:T(1024)S(1)}, f32[1024,1024]{0,1:T(8,128)}) fusion(f32[1024,1024]{0,1:T(8,128)} %copy-done.6, f32[1024]{0:T(1024)S(1)} %convert_element_type.97, f32[1024]{0:T(1024)S(1)} %broadcast_multiply_fusion, bf16[1024,4096]{1,0:T(8,128)(2,1)} %all-gather.10.cloned.1.call-done, f32[1024,4096]{1,0:T(8,128)} %fusion.30, ...), kind=kOutput, calls=%fused_computation.36 | convolution fusion | flops 17272143872 | bytes 44068864 | tf_op jit(solution)/shard_map/dot_general | solution.py:183
  330.1 4.7 fusion.65
  334.8 3.7 fusion.41.g_ref
  338.6 39.8 %shard_map.244 = (bf16[1024,1024]{1,0:T(8,128)(2,1)}, bf16[1024,1024]{1,0:T(8,128)(2,1)}, bf16[1024,1024]{1,0:T(8,128)(2,1)}, f32[16,1024]{1,0:T(8,128)}, f32[16,1024]{1,0:T(8,128)}) custom-call(s32[1040,1]{1,0:T(8,128)} %broadcast_in_dim.27.sc_ref, s32[1,1024]{1,0:T(1,128)} %bitcast.30, bf16[1024,3072]{1,0:T(8,128)(2,1)} %add_convert_fusion.q_ref.k_ref.v_ref, ...), custom_call_target="tpu_custom_call" | custom-call | flops 10737418240 | bytes 16777216 | tf_op jit(solution)/shard_map/pallas_call | solution.py:139
  379.3 40.2 %psum.7 = bf16[10,2048]{1,0:T(8,128)(2,1)S(1)} all-reduce(f32[10,2048]{1,0:T(8,128)S(1)} %pad_maximum_fusion), channel_id=1, replica_groups=mesh['dp'=8,'fsdp'=4] {'dp','fsdp'}, use_global_device_ids=true, to_apply=%region_8.9 | all-reduce | flops 20480 | bytes 122880 | tf_op jit(solution)/shard_map/psum | solution.py:278
  419.5 2.7 fusion.47
  422.2 1.2 convert_reduce_fusion.2
  423.5 1.8 convolution_bitcast_fusion
  425.3 1.0 fusion.69
  426.9 2.9 copy.48
  429.8 11.2 %fusion.24 = (f32[1024]{0:T(1024)S(1)}, f32[1024,1024]{0,1:T(8,128)S(1)}) fusion(bf16[1024,1024]{0,1:T(8,128)(2,1)} %copy.41, f32[1024]{0:T(1024)S(1)} %convert_element_type.87, f32[1024]{0:T(1024)S(1)} %broadcast_multiply_fusion.1, bf16[1024,3072]{1,0:T(8,128)(2,1)} %all-gather.6.cloned.1.call-done, bf16[1024,1024]{1,0:T(8,128)(2,1)} %get-tuple-element.18, ...), kind=kOutput, calls=%fused_computation.32 | convolution fusion | flops 6466567168 | bytes 18886656 | tf_op jit(solution)/shard_map/dot_general | solution.py:183
  441.1 1.1 fusion.46
  442.3 1.0 copy-done.8
  443.9 3.5 add_convert_fusion.1
  447.4 3.9 copy.47
  451.3 17.5 %add_convert_fusion.2 = bf16[1024,1024]{0,1:T(8,128)(2,1)} fusion(f32[1024,1024]{0,1:T(8,128)} %copy-done.6, f32[1024]{0:T(1024)S(1)} %copy-done.17, bf16[4096,1024]{1,0:T(8,128)(2,1)} %all-gather.12.cloned.1.call-done, f32[1024,4096]{1,0:T(8,128)} %fusion.30, f32[4096]{0:T(1024)S(1)} %bitcast.33), kind=kOutput, calls=%fused_computation.37 | convolution fusion | flops 8635023360 | bytes 31477760 | tf_op jit(solution)/shard_map/dot_general | solution.py:173
  468.8 3.9 copy.46
  (93 shorter events, 14.4 us)
Async XLA Ops:
  7.2 128.8 %copy-start = (bf16[512,2048]{1,0:T(8,128)(2,1)S(1)}, bf16[512,2048]{1,0:T(8,128)(2,1)}, u32[]{:S(2)}) copy-start(bf16[512,2048]{1,0:T(8,128)(2,1)} %param.38) | copy-start | bytes 6291460
  7.2 55.5 %copy-start.18 = (bf16[512]{0:T(512)(128)(2,1)S(1)}, bf16[512]{0:T(512)(128)(2,1)}, u32[]{:S(2)}) copy-start(bf16[512]{0:T(512)(128)(2,1)} %param.37) | copy-start | bytes 3076
  7.2 55.5 %copy-start.16 = (bf16[2048]{0:T(1024)(128)(2,1)S(1)}, bf16[2048]{0:T(1024)(128)(2,1)}, u32[]{:S(2)}) copy-start(bf16[2048]{0:T(1024)(128)(2,1)} %param.39) | copy-start | bytes 12292
  7.2 55.5 %copy-start.13 = (s32[1024]{0:T(1024)S(1)}, s32[1024]{0:T(1024)}, u32[]{:S(2)}) copy-start(s32[1024]{0:T(1024)} %param.21) | copy-start | bytes 12292
  7.2 55.9 %copy-start.19 = (bf16[128]{0:T(256)(128)(2,1)S(1)}, bf16[128]{0:T(256)(128)(2,1)}, u32[]{:S(2)}) copy-start(bf16[128]{0:T(256)(128)(2,1)} %param.32) | copy-start | bytes 772
  7.2 130.8 %all-gather.6.cloned.1.call-start = ((), (), s32[]{:S(2)}) async-start(), calls=%async_computation | async-start | bytes 6488064 | tf_op jit(solution)/shard_map/all_gather | solution.py:224
  8.0 173.5 %all-gather.8.cloned.1.call-start = ((), (), s32[]{:S(2)}) async-start(), calls=%async_computation.1 | async-start | bytes 2162688 | tf_op jit(solution)/shard_map/all_gather | solution.py:226
  8.7 212.0 %all-gather.10.cloned.1.call-start = ((), (), s32[]{:S(2)}) async-start(), calls=%async_computation.2 | async-start | bytes 8650752 | tf_op jit(solution)/shard_map/all_gather | solution.py:232
  9.4 290.1 %all-gather.12.cloned.1.call-start = ((), (), s32[]{:S(2)}) async-start(), calls=%async_computation.3 | async-start | bytes 8650752 | tf_op jit(solution)/shard_map/all_gather | solution.py:234
  58.5 76.0 %copy-start.12 = (bf16[10,1024]{1,0:T(8,128)(2,1)S(1)}, bf16[10,1024]{1,0:T(8,128)(2,1)}, u32[]{:S(2)}) copy-start(bf16[10,1024]{1,0:T(8,128)(2,1)} %param.35) | copy-start | bytes 61444
  132.9 3.5 copy-start.4
  136.4 13.9 %copy-start.1 = (bf16[16,2048]{1,0:T(8,128)(2,1)}, bf16[16,2048]{1,0:T(8,128)(2,1)S(1)}, u32[]{:S(2)}) copy-start(bf16[16,2048]{1,0:T(8,128)(2,1)S(1)} %pad.5.pk_ref.pv_ref) | copy-start | bytes 196612
  137.4 0.6 copy-start.14
  178.8 1.3 copy-start.2
  180.1 1.3 copy-start.3
  187.2 1.9 copy-start.6
  330.1 4.7 copy-start.9
  330.1 4.7 copy-start.20
  334.8 3.8 copy-start.7
  419.5 5.8 %copy-start.11 = (bf16[1024,512]{1,0:T(8,128)(2,1)S(1)}, bf16[1024,512]{1,0:T(8,128)(2,1)}, u32[]{:S(2)}) copy-start(bf16[1024,512]{1,0:T(8,128)(2,1)} %param.36) | copy-start | bytes 3145732
  429.8 11.3 %copy-start.15 = (f32[1024]{0:T(1024)S(1)}, f32[1024]{0:T(1024)}, u32[]{:S(2)}) copy-start(f32[1024]{0:T(1024)} %copy-done.14) | copy-start | bytes 12292
  429.8 11.3 %copy-start.5 = (bf16[1024,1024]{0,1:T(8,128)(2,1)S(1)}, bf16[1024,1024]{0,1:T(8,128)(2,1)}, u32[]{:S(2)}) copy-start(bf16[1024,1024]{0,1:T(8,128)(2,1)} %copy.41) | copy-start | bytes 6291460
  441.1 2.2 copy-start.8
  441.1 2.9 copy-start.10
  447.4 3.9 copy-start.17
Sparse Core Ops, SparseCore 0:
  10.9 72.5 all-gather.5
  86.5 54.9 all-gather.7
  144.4 76.2 all-gather.9
  223.5 75.9 all-gather.11
